TPU v7x, 32 devices: a whole 2x2x4 slice. The times are simulated.
32 devices in a mesh: row: 8 (over z, x), col: 4 (over y, core).
Axes of the slice: x: 2, y: 2, z: 4, core: 2. Of those that a mesh axis runs over, the one named last changes fastest.
Arguments:
- records: bfloat16 [128, 8, 1500], P('row', 'col'), may hold values from -6 to 6
- channel_live: int32 [128], replicated, may hold values 0 or 1
- minute_valid: int32 [8], replicated, may hold values 0 or 1
Outputs:
- correlations: bfloat16 [128, 128, 801], P('row', 'col')
All inputs are finite; a program needn't handle non-finite values.
Results may differ from a plain program's by a relative error of at most 0.0075.
Values may be sent and summed in bfloat16 or wider, within the bound.
A program may use at most 64 MiB of HBM per device.

v0:
```python
import math
import jax
import jax.numpy as jnp
from jax import lax
from jax.sharding import PartitionSpec as P

F = 640
BAND = 32
MAXLAG = 400


def forward_table(length, nfreq):
    times = jnp.arange(length, dtype=jnp.int32)[:, None]
    freqs = jnp.arange(1, nfreq + 1, dtype=jnp.int32)[None, :]
    phase = (times * freqs % length).astype(jnp.float32) * jnp.float32(2.0 * math.pi / length)
    return jnp.concatenate([jnp.cos(phase), -jnp.sin(phase)], axis=1).astype(jnp.bfloat16)


def inverse_table(length, nfreq, maxlag):
    freqs = jnp.arange(1, nfreq + 1, dtype=jnp.int32)[:, None]
    shifts = jnp.arange(-maxlag, maxlag + 1, dtype=jnp.int32)[None, :]
    phase = jnp.mod(freqs * shifts, length).astype(jnp.float32) * jnp.float32(
        2.0 * math.pi / length
    )
    return jnp.concatenate([jnp.cos(phase), -jnp.sin(phase)], axis=0).astype(jnp.bfloat16)


def whiten(signal, live, valid, table, band):
    chans, mins, length = signal.shape
    nfreq = table.shape[1] // 2
    spectrum = jnp.dot(
        signal.reshape(chans * mins, length), table, preferred_element_type=jnp.float32
    )
    grouped = spectrum.reshape(chans, mins, 2, nfreq // band, band)
    power = jnp.mean(grouped * grouped, axis=(2, 4))
    weight = (
        lax.rsqrt(power + 1e-06)
        * live.astype(jnp.float32)[:, None, None]
        * valid.astype(jnp.float32)[None, :, None]
    )
    return (
        (grouped * weight[:, :, None, :, None]).reshape(chans, mins, 2 * nfreq).astype(jnp.bfloat16)
    )


def correlate(rows, cols, itab, count):
    nfreq = rows.shape[2] // 2
    row_real = rows[:, :, :nfreq]
    row_imag = rows[:, :, nfreq:]
    col_real = cols[:, :, :nfreq]
    col_imag = cols[:, :, nfreq:]
    real_sum = jnp.einsum(
        "imf,jmf->ijf", row_real, col_real, preferred_element_type=jnp.float32
    ) + jnp.einsum("imf,jmf->ijf", row_imag, col_imag, preferred_element_type=jnp.float32)
    imag_sum = jnp.einsum(
        "imf,jmf->ijf", row_imag, col_real, preferred_element_type=jnp.float32
    ) - jnp.einsum("imf,jmf->ijf", row_real, col_imag, preferred_element_type=jnp.float32)
    stacked = (jnp.concatenate([real_sum, imag_sum], axis=-1) / jnp.float32(count)).astype(
        jnp.bfloat16
    )
    lagged = jnp.dot(stacked.reshape(-1, 2 * nfreq), itab, preferred_element_type=jnp.float32)
    lagged = lagged * jnp.float32(1.0 / math.sqrt(nfreq))
    return lagged.astype(jnp.bfloat16).reshape(rows.shape[0], cols.shape[0], itab.shape[1])


def body(records, channel_live, minute_valid):
    row_total = lax.axis_size("row")
    col_total = lax.axis_size("col")
    row_count = records.shape[0]
    per_device = records.shape[1]
    length = records.shape[2]
    channels = row_count * row_total
    col_count = channels // col_total
    minutes = per_device * col_total
    col_index = lax.axis_index("col")
    row_start = lax.axis_index("row") * row_count
    row_live = lax.dynamic_slice_in_dim(channel_live, row_start, row_count)
    table = forward_table(length, F)
    own_valid = lax.dynamic_slice_in_dim(minute_valid, col_index * per_device, per_device)
    local = whiten(records, row_live, own_valid, table, BAND)
    row_spectra = lax.all_gather(local, "col", axis=1, tiled=True)
    every_channel = lax.all_gather(local, "row", axis=0, tiled=True)
    col_spectra = lax.all_to_all(every_channel, "col", split_axis=0, concat_axis=1, tiled=True)
    itab = inverse_table(length, F, MAXLAG)
    block = math.gcd(row_count, 8)
    grouped = row_spectra.reshape(row_count // block, block, minutes, 2 * F)

    def one_block(rows):
        return correlate(rows, col_spectra, itab, minutes)

    result = lax.map(one_block, grouped)
    return result.reshape(row_count, col_count, 2 * MAXLAG + 1)


def solution(mesh):
    in_specs = (P("row", "col", None), P(), P())
    out_specs = P("row", "col", None)
    return jax.shard_map(body, mesh=mesh, in_specs=in_specs, out_specs=out_specs, check_vma=False)
```

profile of v0, /device:TPU:0, one launch (start us, length us, event | category | flops | bytes accessed | tf_op | source)
XLA Modules:
  0.0 129.4 jit_solution(9751996412103795063)
XLA Ops:
  0.0 17.2 %cosine_convert_fusion = (bf16[1500,640]{1,0:T(8,128)(2,1)S(1)}, bf16[1500,640]{1,0:T(8,128)(2,1)}) fusion(s32[640]{0:T(1024)S(1)} %iota_add_fusion.1), kind=kLoop, calls=%fused_computation.31 | loop fusion | flops 11520000 | bytes 3842560 | tf_op jit(solution)/shard_map/convert.2
  17.2 0.0 copy-done.5
  17.2 0.1 reshape.42
  17.3 0.0 copy-start.8
  17.3 0.0 copy-start.9
  17.3 2.3 %fusion.45 = (f32[32,1280]{1,0:T(8,128)S(1)}, f32[32,1280]{1,0:T(8,128)S(1)}) fusion(bf16[32,1500]{1,0:T(8,128)(2,1)S(1)} %reshape.42, bf16[1500,640]{1,0:T(8,128)(2,1)} %get-tuple-element.61, bf16[1500,640]{1,0:T(8,128)(2,1)S(1)} %get-tuple-element.60), kind=kOutput, calls=%fused_computation.59 | convolution fusion | flops 130600960 | bytes 4263680 | tf_op jit(solution)/shard_map/dot_general | solution.py:31
  19.6 0.3 mul.110
  19.9 0.1 dynamic-slice_convert_fusion.1
  20.0 0.1 dynamic-slice_convert_fusion
  20.0 0.2 reduce_sum.9
  20.2 0.1 fusion.43
  20.3 0.2 mul.117
  20.5 0.3 mul.118
  20.8 0.1 reshape.43
  20.9 33.5 %all_gather.7 = bf16[128,2,1280]{2,0,1:T(8,128)(2,1)S(1)} all-gather(bf16[16,2,1280]{2,0,1:T(8,128)(2,1)S(1)} %fusion.39), channel_id=1, replica_groups=mesh['row'=8,'col'=4] {'row'}, dimensions={0}, use_global_device_ids=true | all-gather | bytes 737280 | tf_op jit(solution)/shard_map/all_gather | solution.py:82
  54.4 1.5 %copy.28 = bf16[128,2,1280]{2,1,0:T(2,128)(2,1)} copy(bf16[128,2,1280]{2,0,1:T(8,128)(2,1)S(1)} %all_gather.7) | data formatting | bytes 1310720 | tf_op jit(solution)/shard_map/all_gather | solution.py:82
  55.9 3.5 %all-to-all-start = ((bf16[128,2,1280]{2,1,0:T(2,128)(2,1)}), bf16[128,2,1280]{2,1,0:T(2,128)(2,1)S(1)}, u32[]{:S(2)}, u32[]{:S(2)}) async-start(bf16[128,2,1280]{2,1,0:T(2,128)(2,1)} %copy.28), calls=%async_computation | async-start | bytes 1310720 | tf_op jit(solution)/shard_map/all_to_all | solution.py:83
  59.4 10.2 %cosine_convert_fusion.1 = (bf16[640,801]{1,0:T(8,128)(2,1)S(1)}, bf16[640,801]{1,0:T(8,128)(2,1)S(1)}) fusion(s32[801]{0:T(1024)S(1)} %iota_add_fusion, s32[640]{0:T(1024)S(1)} %iota_add_fusion.1), kind=kLoop, calls=%fused_computation.41 | loop fusion | flops 6151680 | bytes 2056324 | tf_op jit(solution)/shard_map/convert
  69.6 6.8 %all_gather.6 = bf16[16,8,1280]{2,0,1:T(8,128)(2,1)S(1)} all-gather(bf16[16,2,1280]{2,0,1:T(8,128)(2,1)S(1)} %fusion.39), channel_id=1, replica_groups=mesh['row'=8,'col'=4] {'col'}, dimensions={1}, use_global_device_ids=true | all-gather | bytes 409600 | tf_op jit(solution)/shard_map/all_gather | solution.py:81
  76.4 1.6 %pad_maximum_fusion = bf16[1280,801]{1,0:T(8,128)(2,1)} fusion(bf16[640,801]{1,0:T(8,128)(2,1)S(1)} %get-tuple-element.59, bf16[640,801]{1,0:T(8,128)(2,1)S(1)} %get-tuple-element.58), kind=kLoop, calls=%fused_computation.39 | loop fusion | flops 4101120 | bytes 4101120 | tf_op jit(solution)/shard_map/concatenate | solution.py:25
  78.0 0.0 all-to-all-done
  78.0 4.9 %copy.29 = bf16[32,4,2,1280]{0,2,1,3:T(2,128)(2,1)} copy(bf16[32,4,2,1280]{3,2,0,1:T(2,128)(2,1)S(1)} %bitcast.75) | data formatting | bytes 1310720 | tf_op jit(solution)/shard_map/all_to_all | solution.py:83
  82.9 46.5 %while.10 = (s32[]{:T(128)}, bf16[2,8,32,801]{3,2,1,0:T(8,128)(2,1)}, bf16[2,8,8,1280]{3,1,0,2:T(8,128)(2,1)S(1)}, bf16[32,8,1280]{0,1,2:T(8,128)(2,1)}, bf16[1280,801]{1,0:T(8,128)(2,1)}, /*index=5*/s32[]{:T(128)}) while((s32[]{:T(128)}, bf16[2,8,32,801]{3,2,1,0:T(8,128)(2,1)}, bf16[2,8,8,1280]{3,1,0,2:T(8,128)(2,1)S(1)}, ...), condition=%wide.region_2.3_spmd, body=%wide.region_1.2_spmd.sunk | while | flops 537149952 | bytes 34353424 | solution.py:91
  82.9 0.8 copy-done.3
  83.7 1.8 %copy.50 = bf16[1,8,8,1280]{2,1,3,0:T(8,128)(2,1)S(1)} copy(bf16[1,8,8,1280]{3,1,0,2:T(8,128)(2,1)S(1)} %constant_dynamic-slice_fusion.2) | data formatting | bytes 327680 | tf_op jit(solution)/shard_map/while/body/jit(dynamic_index_in_dim)/dynamic_slice | solution.py:91
  85.4 1.4 %fusion.98 = bf16[32,8,640]{0,1,2:T(8,128)(2,1)S(1)} fusion(bf16[32,8,1280]{0,1,2:T(8,128)(2,1)} %get-tuple-element.110), kind=kLoop, calls=%fused_computation.15.clone.1.clone.1 | loop fusion | bytes 655360 | tf_op jit(solution)/shard_map/while/body/eval_jaxpr/imf,jmf->ijf/dot_general | solution.py:54
  86.8 0.0 copy-start
  86.8 0.8 fusion.99
  87.7 0.9 copy-done
  88.6 0.1 fusion.100
  88.7 2.4 %add_bitcast_fusion.2 = f32[8,32,640]{1,0,2:T(8,128)} fusion(f32[640,8,32]{2,1,0:T(8,128)S(1)} %fusion.99, bf16[1,8,8,1280]{2,1,3,0:T(8,128)(2,1)S(1)} %copy.50, bf16[32,8,640]{0,1,2:T(8,128)(2,1)S(1)} %fusion.100), kind=kOutput, calls=%fused_computation.9.clone.2 | convolution fusion | flops 2785280 | bytes 1802240 | tf_op jit(solution)/shard_map/while/body/eval_jaxpr/imf,jmf->ijf/dot_general | solution.py:52
  91.0 3.0 %copy.52 = f32[8,32,640]{2,1,0:T(8,128)} copy(f32[8,32,640]{1,0,2:T(8,128)} %add_bitcast_fusion.2) | data formatting | bytes 1310720 | tf_op jit(solution)/shard_map/while/body/eval_jaxpr/add | solution.py:52
  94.1 1.4 %fusion.95 = bf16[32,8,640]{0,1,2:T(8,128)(2,1)S(1)} fusion(bf16[32,8,1280]{0,1,2:T(8,128)(2,1)} %get-tuple-element.110), kind=kLoop, calls=%fused_computation.16.clone.1.clone.1 | loop fusion | bytes 655360 | tf_op jit(solution)/shard_map/while/body/eval_jaxpr/imf,jmf->ijf/dot_general | solution.py:55
  95.5 0.8 fusion.96
  96.3 0.9 copy-done.1
  97.2 0.1 fusion.97
  97.3 2.4 %subtract_bitcast_fusion.2 = f32[8,32,640]{1,0,2:T(8,128)} fusion(f32[640,8,32]{2,1,0:T(8,128)S(1)} %fusion.96, bf16[1,8,8,1280]{2,1,3,0:T(8,128)(2,1)S(1)} %copy.50, bf16[32,8,640]{0,1,2:T(8,128)(2,1)S(1)} %fusion.97), kind=kOutput, calls=%fused_computation.8.clone.2 | convolution fusion | flops 2785280 | bytes 1802240 | tf_op jit(solution)/shard_map/while/body/eval_jaxpr/imf,jmf->ijf/dot_general | solution.py:57
  99.7 2.5 %copy.51 = f32[8,32,640]{2,1,0:T(8,128)S(1)} copy(f32[8,32,640]{1,0,2:T(8,128)} %subtract_bitcast_fusion.2) | data formatting | bytes 1310720 | tf_op jit(solution)/shard_map/while/body/eval_jaxpr/sub | solution.py:55
  102.2 0.0 copy-start.6
  102.2 2.7 %fusion.101 = bf16[256,801]{0,1:T(8,128)(2,1)S(1)} fusion(bf16[1280,801]{1,0:T(8,128)(2,1)} %get-tuple-element.111, f32[256,640]{1,0:T(8,128)S(1)} %bitcast.73, f32[256,640]{1,0:T(8,128)S(1)} %bitcast.72), kind=kOutput, calls=%fused_computation.13.clone.1 | convolution fusion | flops 526336512 | bytes 3771392 | tf_op jit(solution)/shard_map/while/body/eval_jaxpr/dot_general | solution.py:61
  104.9 0.2 copy.53
  105.2 0.1 constant_dynamic-update-slice_fusion.2
  105.2 0.0 copy-start.7
  105.2 0.9 copy-done.7
  106.2 0.8 copy-done.3
  106.9 1.8 %copy.50 = bf16[1,8,8,1280]{2,1,3,0:T(8,128)(2,1)S(1)} copy(bf16[1,8,8,1280]{3,1,0,2:T(8,128)(2,1)S(1)} %constant_dynamic-slice_fusion.2) | data formatting | bytes 327680 | tf_op jit(solution)/shard_map/while/body/jit(dynamic_index_in_dim)/dynamic_slice | solution.py:91
  108.7 1.4 %fusion.98 = bf16[32,8,640]{0,1,2:T(8,128)(2,1)S(1)} fusion(bf16[32,8,1280]{0,1,2:T(8,128)(2,1)} %get-tuple-element.110), kind=kLoop, calls=%fused_computation.15.clone.1.clone.1 | loop fusion | bytes 655360 | tf_op jit(solution)/shard_map/while/body/eval_jaxpr/imf,jmf->ijf/dot_general | solution.py:54
  110.1 0.8 fusion.99
  110.9 0.9 copy-done
  111.8 0.1 fusion.100
  111.9 2.4 %add_bitcast_fusion.2 = f32[8,32,640]{1,0,2:T(8,128)} fusion(f32[640,8,32]{2,1,0:T(8,128)S(1)} %fusion.99, bf16[1,8,8,1280]{2,1,3,0:T(8,128)(2,1)S(1)} %copy.50, bf16[32,8,640]{0,1,2:T(8,128)(2,1)S(1)} %fusion.100), kind=kOutput, calls=%fused_computation.9.clone.2 | convolution fusion | flops 2785280 | bytes 1802240 | tf_op jit(solution)/shard_map/while/body/eval_jaxpr/imf,jmf->ijf/dot_general | solution.py:52
  114.3 3.0 %copy.52 = f32[8,32,640]{2,1,0:T(8,128)} copy(f32[8,32,640]{1,0,2:T(8,128)} %add_bitcast_fusion.2) | data formatting | bytes 1310720 | tf_op jit(solution)/shard_map/while/body/eval_jaxpr/add | solution.py:52
  117.3 1.4 %fusion.95 = bf16[32,8,640]{0,1,2:T(8,128)(2,1)S(1)} fusion(bf16[32,8,1280]{0,1,2:T(8,128)(2,1)} %get-tuple-element.110), kind=kLoop, calls=%fused_computation.16.clone.1.clone.1 | loop fusion | bytes 655360 | tf_op jit(solution)/shard_map/while/body/eval_jaxpr/imf,jmf->ijf/dot_general | solution.py:55
  118.7 0.8 fusion.96
  119.6 0.9 copy-done.1
  120.5 0.1 fusion.97
  120.6 2.4 %subtract_bitcast_fusion.2 = f32[8,32,640]{1,0,2:T(8,128)} fusion(f32[640,8,32]{2,1,0:T(8,128)S(1)} %fusion.96, bf16[1,8,8,1280]{2,1,3,0:T(8,128)(2,1)S(1)} %copy.50, bf16[32,8,640]{0,1,2:T(8,128)(2,1)S(1)} %fusion.97), kind=kOutput, calls=%fused_computation.8.clone.2 | convolution fusion | flops 2785280 | bytes 1802240 | tf_op jit(solution)/shard_map/while/body/eval_jaxpr/imf,jmf->ijf/dot_general | solution.py:57
  122.9 2.5 %copy.51 = f32[8,32,640]{2,1,0:T(8,128)S(1)} copy(f32[8,32,640]{1,0,2:T(8,128)} %subtract_bitcast_fusion.2) | data formatting | bytes 1310720 | tf_op jit(solution)/shard_map/while/body/eval_jaxpr/sub | solution.py:55
  125.4 0.0 copy-start.6
  125.5 2.7 %fusion.101 = bf16[256,801]{0,1:T(8,128)(2,1)S(1)} fusion(bf16[1280,801]{1,0:T(8,128)(2,1)} %get-tuple-element.111, f32[256,640]{1,0:T(8,128)S(1)} %bitcast.73, f32[256,640]{1,0:T(8,128)S(1)} %bitcast.72), kind=kOutput, calls=%fused_computation.13.clone.1 | convolution fusion | flops 526336512 | bytes 3771392 | tf_op jit(solution)/shard_map/while/body/eval_jaxpr/dot_general | solution.py:61
  128.2 0.2 copy.53
  128.4 0.1 constant_dynamic-update-slice_fusion.2
  128.5 0.0 copy-start.7
  128.5 0.9 copy-done.7
  (24 shorter events, 0.1 us)
Async XLA Ops:
  0.0 17.2 %copy-start.5 = (bf16[16,2,1500]{2,1,0:T(2,128)(2,1)S(1)}, bf16[16,2,1500]{2,1,0:T(2,128)(2,1)}, u32[]{:S(2)}) copy-start(bf16[16,2,1500]{2,1,0:T(2,128)(2,1)} %param.5) | copy-start | bytes 288004
  17.3 2.6 %copy-start.8 = (s32[128]{0:T(128)S(1)}, s32[128]{0:T(128)}, u32[]{:S(2)}) copy-start(s32[128]{0:T(128)} %param.6) | copy-start | bytes 1540
  17.3 2.7 %copy-start.9 = (s32[8]{0:T(128)S(1)}, s32[8]{0:T(128)}, u32[]{:S(2)}) copy-start(s32[8]{0:T(128)} %param.7) | copy-start | bytes 100
  55.9 22.1 %all-to-all-start = ((bf16[128,2,1280]{2,1,0:T(2,128)(2,1)}), bf16[128,2,1280]{2,1,0:T(2,128)(2,1)S(1)}, u32[]{:S(2)}, u32[]{:S(2)}) async-start(bf16[128,2,1280]{2,1,0:T(2,128)(2,1)} %copy.28), calls=%async_computation | async-start | bytes 1310720 | tf_op jit(solution)/shard_map/all_to_all | solution.py:83
  82.9 0.8 copy-start.3
  86.8 1.7 %copy-start = (bf16[32,8,1280]{0,1,2:T(8,128)(2,1)S(1)}, bf16[32,8,1280]{0,1,2:T(8,128)(2,1)}, u32[]{:S(2)}) copy-start(bf16[32,8,1280]{0,1,2:T(8,128)(2,1)} %get-tuple-element.110) | copy-start | bytes 1966084 | tf_op jit(solution)/shard_map/while
  95.5 1.7 %copy-start.1 = (bf16[32,8,1280]{0,1,2:T(8,128)(2,1)S(1)}, bf16[32,8,1280]{0,1,2:T(8,128)(2,1)}, u32[]{:S(2)}) copy-start(bf16[32,8,1280]{0,1,2:T(8,128)(2,1)} %get-tuple-element.110) | copy-start | bytes 1966084 | tf_op jit(solution)/shard_map/while
  99.7 2.5 %copy-start.2 = (f32[8,32,640]{2,1,0:T(8,128)S(1)}, f32[8,32,640]{2,1,0:T(8,128)}, u32[]{:S(2)}) copy-start(f32[8,32,640]{2,1,0:T(8,128)} %copy.52) | copy-start | bytes 1966084 | tf_op jit(solution)/shard_map/while
  102.2 3.0 %copy-start.6 = (bf16[2,8,32,801]{3,2,1,0:T(8,128)(2,1)S(1)}, bf16[2,8,32,801]{3,2,1,0:T(8,128)(2,1)}, u32[]{:S(2)}) copy-start(bf16[2,8,32,801]{3,2,1,0:T(8,128)(2,1)} %get-tuple-element.102) | copy-start | bytes 2460676 | tf_op jit(solution)/shard_map/while
  102.2 4.0 %copy-start.4 = (bf16[2,8,8,1280]{3,1,0,2:T(8,128)(2,1)S(1)}, bf16[2,8,8,1280]{3,1,0,2:T(8,128)(2,1)}, u32[]{:S(2)}) copy-start(bf16[2,8,8,1280]{3,1,0,2:T(8,128)(2,1)} %copy-done.3) | copy-start | bytes 983044 | tf_op jit(solution)/shard_map/while
  105.2 0.9 copy-start.7
  106.2 0.8 copy-start.3
  110.1 1.7 %copy-start = (bf16[32,8,1280]{0,1,2:T(8,128)(2,1)S(1)}, bf16[32,8,1280]{0,1,2:T(8,128)(2,1)}, u32[]{:S(2)}) copy-start(bf16[32,8,1280]{0,1,2:T(8,128)(2,1)} %get-tuple-element.110) | copy-start | bytes 1966084 | tf_op jit(solution)/shard_map/while
  118.7 1.7 %copy-start.1 = (bf16[32,8,1280]{0,1,2:T(8,128)(2,1)S(1)}, bf16[32,8,1280]{0,1,2:T(8,128)(2,1)}, u32[]{:S(2)}) copy-start(bf16[32,8,1280]{0,1,2:T(8,128)(2,1)} %get-tuple-element.110) | copy-start | bytes 1966084 | tf_op jit(solution)/shard_map/while
  122.9 2.5 %copy-start.2 = (f32[8,32,640]{2,1,0:T(8,128)S(1)}, f32[8,32,640]{2,1,0:T(8,128)}, u32[]{:S(2)}) copy-start(f32[8,32,640]{2,1,0:T(8,128)} %copy.52) | copy-start | bytes 1966084 | tf_op jit(solution)/shard_map/while
  125.4 3.0 %copy-start.6 = (bf16[2,8,32,801]{3,2,1,0:T(8,128)(2,1)S(1)}, bf16[2,8,32,801]{3,2,1,0:T(8,128)(2,1)}, u32[]{:S(2)}) copy-start(bf16[2,8,32,801]{3,2,1,0:T(8,128)(2,1)} %get-tuple-element.102) | copy-start | bytes 2460676 | tf_op jit(solution)/shard_map/while
  125.4 4.0 %copy-start.4 = (bf16[2,8,8,1280]{3,1,0,2:T(8,128)(2,1)S(1)}, bf16[2,8,8,1280]{3,1,0,2:T(8,128)(2,1)}, u32[]{:S(2)}) copy-start(bf16[2,8,8,1280]{3,1,0,2:T(8,128)(2,1)} %copy-done.3) | copy-start | bytes 983044 | tf_op jit(solution)/shard_map/while
  128.5 0.9 copy-start.7
where the time goes:
time: 130 us; the launch traced here: 129 us
  blocking collectives  40.2 us (31%)
  local copies, waits for them, and re-layouts  35.4 us (27%)
  other arithmetic  29.5 us (23%)
  matrix products  20.4 us (16%)
  starting transfers between devices  3.48 us (3%)
    all_gather x1, blocking collectives, body(): every_channel = lax.all_gather(local, 'row', axis=0, tiled=True)  33.5 us
    another operation x2, other arithmetic  27.4 us
    while x28, local copies, waits for them, and re-layouts  7.03 us
    all_gather x1, blocking collectives, body(): row_spectra = lax.all_gather(local, 'col', axis=1, tiled=True)  6.76 us
    add x2, local copies, waits for them, and re-layouts, correlate(): jnp.einsum('imf,jmf->ijf', row_real, col_real, preferred_element_type=jnp...  6.06 us
    dot_general x2, matrix products, correlate(): jnp.dot(stacked.reshape(-1, 2 * nfreq), itab, preferred_element_type=jnp....  5.41 us
    sub x2, local copies, waits for them, and re-layouts, correlate(): jnp.einsum('imf,jmf->ijf', row_imag, col_real, preferred_element_type=jnp...  4.94 us
    all_to_all x1, local copies, waits for them, and re-layouts, body(): lax.all_to_all(every_channel, 'col', split_axis=0, concat_axis=1, tiled=T...  4.91 us
  transfers between devices with their start and end apart: 1, of which 0 were waited for; matrix products, arithmetic and copies ran while one was open for 9% of the time, Pallas kernels for 0%

commit v1 on v0

--- a/solution.py
+++ b/solution.py
@@ -78,7 +78,16 @@
     table = forward_table(length, F)
     own_valid = lax.dynamic_slice_in_dim(minute_valid, col_index * per_device, per_device)
     local = whiten(records, row_live, own_valid, table, BAND)
-    row_spectra = lax.all_gather(local, "col", axis=1, tiled=True)
+    size, place, extent = (lax.axis_size("col"), lax.axis_index("col"), local.shape[1])
+    right = [(i, (i + 1) % size) for i in range(size)]
+    result_2 = jnp.zeros((*local.shape[:1], size * extent, *local.shape[1 + 1 :]), local.dtype)
+    held = local
+    for hop in range(size):
+        source = (place - hop) % size
+        result_2 = lax.dynamic_update_slice_in_dim(result_2, held, source * extent, axis=1)
+        if hop < size - 1:
+            held = lax.ppermute(held, "col", right)
+    row_spectra = result_2
     every_channel = lax.all_gather(local, "row", axis=0, tiled=True)
     col_spectra = lax.all_to_all(every_channel, "col", split_axis=0, concat_axis=1, tiled=True)
     itab = inverse_table(length, F, MAXLAG)

time: 130 us -> 131 us (level)
  blocking collectives: 40.2 us -> 33 us
  waiting for transfers between devices: 0.01 us -> 7.07 us
    ppermute x0 -> x3, waiting for transfers between devices: none -> 7.06 us  [body(): held = lax.ppermute(held, 'col', right)]
    all_gather x1 -> x0, blocking collectives: 6.76 us -> none  [body(): row_spectra = lax.all_gather(local, 'col', axis=1, tiled=True)]
  transfers between devices with their start and end apart: 1 -> 4, of which waited for: 0 -> 2; matrix products, arithmetic and copies ran while one was open for 9% -> 11% of each run, Pallas kernels for 0% -> 0%
where the time goes in v1:
time: 131 us
  local copies, waits for them, and re-layouts  35.9 us (27%)
  blocking collectives  33 us (25%)
  other arithmetic  29.5 us (23%)
  matrix products  20.4 us (16%)
  waiting for transfers between devices  7.07 us (5%)
  starting transfers between devices  4.53 us (3%)
    all_gather x1, blocking collectives, body(): every_channel = lax.all_gather(local, 'row', axis=0, tiled=True)  33 us
    another operation x2, other arithmetic  27.4 us
    ppermute x3, waiting for transfers between devices, body(): held = lax.ppermute(held, 'col', right)  7.06 us
    while x28, local copies, waits for them, and re-layouts  7.02 us
    add x2, local copies, waits for them, and re-layouts, correlate(): jnp.einsum('imf,jmf->ijf', row_real, col_real, preferred_element_type=jnp...  6.13 us
    dot_general x2, matrix products, correlate(): jnp.dot(stacked.reshape(-1, 2 * nfreq), itab, preferred_element_type=jnp....  5.41 us
    all_to_all x1, local copies, waits for them, and re-layouts, body(): lax.all_to_all(every_channel, 'col', split_axis=0, concat_axis=1, tiled=T...  4.96 us
    sub x2, local copies, waits for them, and re-layouts, correlate(): jnp.einsum('imf,jmf->ijf', row_imag, col_real, preferred_element_type=jnp...  4.94 us
  transfers between devices with their start and end apart: 4, of which 2 were waited for; matrix products, arithmetic and copies ran while one was open for 11% of the time, Pallas kernels for 0%

profile of v1, /device:TPU:0, one launch (start us, length us, event | category | flops | bytes accessed | tf_op | source)
XLA Modules:
  0.0 130.8 jit_solution(11740698691924445887)
XLA Ops:
  0.0 17.2 %cosine_convert_fusion = (bf16[1500,640]{1,0:T(8,128)(2,1)S(1)}, bf16[1500,640]{1,0:T(8,128)(2,1)}) fusion(s32[640]{0:T(1024)S(1)} %iota_add_fusion.1), kind=kLoop, calls=%fused_computation.31 | loop fusion | flops 11520000 | bytes 3842560 | tf_op jit(solution)/shard_map/convert.2
  17.2 0.1 reshape.42
  17.3 0.0 copy-start.8
  17.3 0.0 copy-start.9
  17.3 2.3 %fusion.45 = (f32[32,1280]{1,0:T(8,128)S(1)}, f32[32,1280]{1,0:T(8,128)S(1)}) fusion(bf16[32,1500]{1,0:T(8,128)(2,1)S(1)} %reshape.42, bf16[1500,640]{1,0:T(8,128)(2,1)} %get-tuple-element.61, bf16[1500,640]{1,0:T(8,128)(2,1)S(1)} %get-tuple-element.60), kind=kOutput, calls=%fused_computation.63 | convolution fusion | flops 130600960 | bytes 4263680 | tf_op jit(solution)/shard_map/dot_general | solution.py:31
  19.6 0.3 mul.122
  19.9 0.1 dynamic-slice_convert_fusion
  20.0 0.1 dynamic-slice_convert_fusion.1
  20.0 0.2 reduce_sum.9
  20.2 0.1 fusion.43
  20.3 0.2 mul.129
  20.5 0.3 mul.130
  20.8 0.1 reshape.43
  20.9 0.6 collective-permute-start
  21.5 33.0 %all_gather.3 = bf16[128,2,1280]{2,0,1:T(8,128)(2,1)S(1)} all-gather(bf16[16,2,1280]{2,0,1:T(8,128)(2,1)S(1)} %fusion.39), channel_id=1, replica_groups=mesh['row'=8,'col'=4] {'row'}, dimensions={0}, use_global_device_ids=true | all-gather | bytes 737280 | tf_op jit(solution)/shard_map/all_gather | solution.py:91
  54.5 1.5 %copy.37 = bf16[128,2,1280]{2,1,0:T(2,128)(2,1)} copy(bf16[128,2,1280]{2,0,1:T(8,128)(2,1)S(1)} %all_gather.3) | data formatting | bytes 1310720 | tf_op jit(solution)/shard_map/all_gather | solution.py:91
  56.0 3.5 %all-to-all-start = ((bf16[128,2,1280]{2,1,0:T(2,128)(2,1)}), bf16[128,2,1280]{2,1,0:T(2,128)(2,1)S(1)}, u32[]{:S(2)}, u32[]{:S(2)}) async-start(bf16[128,2,1280]{2,1,0:T(2,128)(2,1)} %copy.37), calls=%async_computation | async-start | bytes 1310720 | tf_op jit(solution)/shard_map/all_to_all | solution.py:92
  59.5 10.2 %cosine_convert_fusion.1 = (bf16[640,801]{1,0:T(8,128)(2,1)S(1)}, bf16[640,801]{1,0:T(8,128)(2,1)S(1)}) fusion(s32[801]{0:T(1024)S(1)} %iota_add_fusion, s32[640]{0:T(1024)S(1)} %iota_add_fusion.1), kind=kLoop, calls=%fused_computation.41 | loop fusion | flops 6151680 | bytes 2056324 | tf_op jit(solution)/shard_map/convert
  69.8 0.1 copy_dynamic-update-slice_fusion.3
  69.9 1.6 %pad_maximum_fusion = bf16[1280,801]{1,0:T(8,128)(2,1)} fusion(bf16[640,801]{1,0:T(8,128)(2,1)S(1)} %get-tuple-element.59, bf16[640,801]{1,0:T(8,128)(2,1)S(1)} %get-tuple-element.58), kind=kLoop, calls=%fused_computation.39 | loop fusion | flops 4101120 | bytes 4101120 | tf_op jit(solution)/shard_map/concatenate | solution.py:25
  71.5 0.4 collective-permute-start.1
  71.9 0.1 copy_dynamic-update-slice_fusion.2
  72.1 3.3 %collective-permute-done.1 = bf16[16,2,1280]{2,0,1:T(8,128)(2,1)S(1)} collective-permute-done((bf16[16,2,1280]{2,0,1:T(8,128)(2,1)S(1)}, bf16[16,2,1280]{2,0,1:T(8,128)(2,1)S(1)}, u32[]{:S(2)}, u32[]{:S(2)}) %collective-permute-start.1) | collective-permute-done | bytes 81952 | tf_op jit(solution)/shard_map/ppermute | solution.py:89
  75.4 0.1 copy_dynamic-update-slice_fusion.1
  75.5 3.7 %collective-permute-done.2 = bf16[16,2,1280]{2,0,1:T(8,128)(2,1)S(1)} collective-permute-done((bf16[16,2,1280]{2,0,1:T(8,128)(2,1)S(1)}, bf16[16,2,1280]{2,0,1:T(8,128)(2,1)S(1)}, u32[]{:S(2)}, u32[]{:S(2)}) %collective-permute-start.2) | collective-permute-done | bytes 81952 | tf_op jit(solution)/shard_map/ppermute | solution.py:89
  79.2 0.1 copy_dynamic-update-slice_fusion
  79.4 5.0 %copy.38 = bf16[32,4,2,1280]{0,2,1,3:T(2,128)(2,1)} copy(bf16[32,4,2,1280]{3,2,0,1:T(2,128)(2,1)S(1)} %bitcast.75) | data formatting | bytes 1310720 | tf_op jit(solution)/shard_map/all_to_all | solution.py:92
  84.3 46.5 %while.10 = (s32[]{:T(128)}, bf16[2,8,32,801]{3,2,1,0:T(8,128)(2,1)}, bf16[2,8,8,1280]{3,2,1,0:T(8,128)(2,1)S(1)}, bf16[32,8,1280]{0,1,2:T(8,128)(2,1)}, bf16[1280,801]{1,0:T(8,128)(2,1)}, /*index=5*/s32[]{:T(128)}) while((s32[]{:T(128)}, bf16[2,8,32,801]{3,2,1,0:T(8,128)(2,1)}, bf16[2,8,8,1280]{3,2,1,0:T(8,128)(2,1)S(1)}, ...), condition=%wide.region_2.3_spmd, body=%wide.region_1.2_spmd.sunk | while | flops 537149952 | bytes 34353424 | solution.py:100
  84.3 0.8 copy-done.3
  85.1 1.7 %copy.61 = bf16[1,8,8,1280]{2,1,3,0:T(8,128)(2,1)S(1)} copy(bf16[1,8,8,1280]{3,2,1,0:T(8,128)(2,1)S(1)} %constant_dynamic-slice_fusion.2) | data formatting | bytes 327680 | tf_op jit(solution)/shard_map/while/body/jit(dynamic_index_in_dim)/dynamic_slice | solution.py:100
  86.8 1.4 %fusion.98 = bf16[32,8,640]{0,1,2:T(8,128)(2,1)S(1)} fusion(bf16[32,8,1280]{0,1,2:T(8,128)(2,1)} %get-tuple-element.110), kind=kLoop, calls=%fused_computation.15.clone.1.clone.1 | loop fusion | bytes 655360 | tf_op jit(solution)/shard_map/while/body/eval_jaxpr/imf,jmf->ijf/dot_general | solution.py:54
  88.2 0.8 fusion.99
  89.1 0.9 copy-done
  90.0 0.1 fusion.100
  90.1 2.4 %add_bitcast_fusion.2 = f32[8,32,640]{1,0,2:T(8,128)} fusion(f32[640,8,32]{2,1,0:T(8,128)S(1)} %fusion.99, bf16[1,8,8,1280]{2,1,3,0:T(8,128)(2,1)S(1)} %copy.61, bf16[32,8,640]{0,1,2:T(8,128)(2,1)S(1)} %fusion.100), kind=kOutput, calls=%fused_computation.9.clone.2 | convolution fusion | flops 2785280 | bytes 1802240 | tf_op jit(solution)/shard_map/while/body/eval_jaxpr/imf,jmf->ijf/dot_general | solution.py:52
  92.4 3.1 %copy.63 = f32[8,32,640]{2,1,0:T(8,128)} copy(f32[8,32,640]{1,0,2:T(8,128)} %add_bitcast_fusion.2) | data formatting | bytes 1310720 | tf_op jit(solution)/shard_map/while/body/eval_jaxpr/add | solution.py:52
  95.5 1.4 %fusion.95 = bf16[32,8,640]{0,1,2:T(8,128)(2,1)S(1)} fusion(bf16[32,8,1280]{0,1,2:T(8,128)(2,1)} %get-tuple-element.110), kind=kLoop, calls=%fused_computation.16.clone.1.clone.1 | loop fusion | bytes 655360 | tf_op jit(solution)/shard_map/while/body/eval_jaxpr/imf,jmf->ijf/dot_general | solution.py:55
  96.9 0.8 fusion.96
  97.7 0.9 copy-done.1
  98.6 0.1 fusion.97
  98.7 2.4 %subtract_bitcast_fusion.2 = f32[8,32,640]{1,0,2:T(8,128)} fusion(f32[640,8,32]{2,1,0:T(8,128)S(1)} %fusion.96, bf16[1,8,8,1280]{2,1,3,0:T(8,128)(2,1)S(1)} %copy.61, bf16[32,8,640]{0,1,2:T(8,128)(2,1)S(1)} %fusion.97), kind=kOutput, calls=%fused_computation.8.clone.2 | convolution fusion | flops 2785280 | bytes 1802240 | tf_op jit(solution)/shard_map/while/body/eval_jaxpr/imf,jmf->ijf/dot_general | solution.py:57
  101.1 2.5 %copy.62 = f32[8,32,640]{2,1,0:T(8,128)S(1)} copy(f32[8,32,640]{1,0,2:T(8,128)} %subtract_bitcast_fusion.2) | data formatting | bytes 1310720 | tf_op jit(solution)/shard_map/while/body/eval_jaxpr/sub | solution.py:55
  103.6 2.7 %fusion.101 = bf16[256,801]{0,1:T(8,128)(2,1)S(1)} fusion(bf16[1280,801]{1,0:T(8,128)(2,1)} %get-tuple-element.111, f32[256,640]{1,0:T(8,128)S(1)} %bitcast.73, f32[256,640]{1,0:T(8,128)S(1)} %bitcast.72), kind=kOutput, calls=%fused_computation.13.clone.1 | convolution fusion | flops 526336512 | bytes 3771392 | tf_op jit(solution)/shard_map/while/body/eval_jaxpr/dot_general | solution.py:61
  106.3 0.2 copy.64
  106.6 0.1 constant_dynamic-update-slice_fusion.2
  106.7 0.9 copy-done.7
  107.6 0.8 copy-done.3
  108.4 1.7 %copy.61 = bf16[1,8,8,1280]{2,1,3,0:T(8,128)(2,1)S(1)} copy(bf16[1,8,8,1280]{3,2,1,0:T(8,128)(2,1)S(1)} %constant_dynamic-slice_fusion.2) | data formatting | bytes 327680 | tf_op jit(solution)/shard_map/while/body/jit(dynamic_index_in_dim)/dynamic_slice | solution.py:100
  110.1 1.4 %fusion.98 = bf16[32,8,640]{0,1,2:T(8,128)(2,1)S(1)} fusion(bf16[32,8,1280]{0,1,2:T(8,128)(2,1)} %get-tuple-element.110), kind=kLoop, calls=%fused_computation.15.clone.1.clone.1 | loop fusion | bytes 655360 | tf_op jit(solution)/shard_map/while/body/eval_jaxpr/imf,jmf->ijf/dot_general | solution.py:54
  111.5 0.8 fusion.99
  112.3 0.9 copy-done
  113.2 0.1 fusion.100
  113.3 2.4 %add_bitcast_fusion.2 = f32[8,32,640]{1,0,2:T(8,128)} fusion(f32[640,8,32]{2,1,0:T(8,128)S(1)} %fusion.99, bf16[1,8,8,1280]{2,1,3,0:T(8,128)(2,1)S(1)} %copy.61, bf16[32,8,640]{0,1,2:T(8,128)(2,1)S(1)} %fusion.100), kind=kOutput, calls=%fused_computation.9.clone.2 | convolution fusion | flops 2785280 | bytes 1802240 | tf_op jit(solution)/shard_map/while/body/eval_jaxpr/imf,jmf->ijf/dot_general | solution.py:52
  115.7 3.1 %copy.63 = f32[8,32,640]{2,1,0:T(8,128)} copy(f32[8,32,640]{1,0,2:T(8,128)} %add_bitcast_fusion.2) | data formatting | bytes 1310720 | tf_op jit(solution)/shard_map/while/body/eval_jaxpr/add | solution.py:52
  118.7 1.4 %fusion.95 = bf16[32,8,640]{0,1,2:T(8,128)(2,1)S(1)} fusion(bf16[32,8,1280]{0,1,2:T(8,128)(2,1)} %get-tuple-element.110), kind=kLoop, calls=%fused_computation.16.clone.1.clone.1 | loop fusion | bytes 655360 | tf_op jit(solution)/shard_map/while/body/eval_jaxpr/imf,jmf->ijf/dot_general | solution.py:55
  120.2 0.8 fusion.96
  121.0 0.9 copy-done.1
  121.9 0.1 fusion.97
  122.0 2.4 %subtract_bitcast_fusion.2 = f32[8,32,640]{1,0,2:T(8,128)} fusion(f32[640,8,32]{2,1,0:T(8,128)S(1)} %fusion.96, bf16[1,8,8,1280]{2,1,3,0:T(8,128)(2,1)S(1)} %copy.61, bf16[32,8,640]{0,1,2:T(8,128)(2,1)S(1)} %fusion.97), kind=kOutput, calls=%fused_computation.8.clone.2 | convolution fusion | flops 2785280 | bytes 1802240 | tf_op jit(solution)/shard_map/while/body/eval_jaxpr/imf,jmf->ijf/dot_general | solution.py:57
  124.4 2.5 %copy.62 = f32[8,32,640]{2,1,0:T(8,128)S(1)} copy(f32[8,32,640]{1,0,2:T(8,128)} %subtract_bitcast_fusion.2) | data formatting | bytes 1310720 | tf_op jit(solution)/shard_map/while/body/eval_jaxpr/sub | solution.py:55
  126.9 2.7 %fusion.101 = bf16[256,801]{0,1:T(8,128)(2,1)S(1)} fusion(bf16[1280,801]{1,0:T(8,128)(2,1)} %get-tuple-element.111, f32[256,640]{1,0:T(8,128)S(1)} %bitcast.73, f32[256,640]{1,0:T(8,128)S(1)} %bitcast.72), kind=kOutput, calls=%fused_computation.13.clone.1 | convolution fusion | flops 526336512 | bytes 3771392 | tf_op jit(solution)/shard_map/while/body/eval_jaxpr/dot_general | solution.py:61
  129.6 0.2 copy.64
  129.8 0.1 constant_dynamic-update-slice_fusion.2
  129.9 0.9 copy-done.7
  (34 shorter events, 0.1 us)
Async XLA Ops:
  0.0 17.2 %copy-start.5 = (bf16[16,2,1500]{2,1,0:T(2,128)(2,1)S(1)}, bf16[16,2,1500]{2,1,0:T(2,128)(2,1)}, u32[]{:S(2)}) copy-start(bf16[16,2,1500]{2,1,0:T(2,128)(2,1)} %param.5) | copy-start | bytes 288004
  17.3 2.6 %copy-start.8 = (s32[8]{0:T(128)S(1)}, s32[8]{0:T(128)}, u32[]{:S(2)}) copy-start(s32[8]{0:T(128)} %param.7) | copy-start | bytes 100
  17.3 2.7 %copy-start.9 = (s32[128]{0:T(128)S(1)}, s32[128]{0:T(128)}, u32[]{:S(2)}) copy-start(s32[128]{0:T(128)} %param.6) | copy-start | bytes 1540
  20.9 50.6 %collective-permute-start = (bf16[16,2,1280]{2,0,1:T(8,128)(2,1)S(1)}, bf16[16,2,1280]{2,0,1:T(8,128)(2,1)S(1)}, u32[]{:S(2)}, u32[]{:S(2)}) collective-permute-start(bf16[16,2,1280]{2,0,1:T(8,128)(2,1)S(1)} %fusion.39), channel_id=1, source_target_pairs={{0,1},{1,2},{2,3},{3,0},{4,5},{5,6},{6,7},{7,4},{8,9},{9,10},{10,1... | collective-permute-start | bytes 245768 | tf_op jit(solution)/shard_map/ppermute | solution.py:89
  56.0 23.3 %all-to-all-start = ((bf16[128,2,1280]{2,1,0:T(2,128)(2,1)}), bf16[128,2,1280]{2,1,0:T(2,128)(2,1)S(1)}, u32[]{:S(2)}, u32[]{:S(2)}) async-start(bf16[128,2,1280]{2,1,0:T(2,128)(2,1)} %copy.37), calls=%async_computation | async-start | bytes 1310720 | tf_op jit(solution)/shard_map/all_to_all | solution.py:92
  71.5 3.9 %collective-permute-start.1 = (bf16[16,2,1280]{2,0,1:T(8,128)(2,1)S(1)}, bf16[16,2,1280]{2,0,1:T(8,128)(2,1)S(1)}, u32[]{:S(2)}, u32[]{:S(2)}) collective-permute-start(bf16[16,2,1280]{2,0,1:T(8,128)(2,1)S(1)} %collective-permute-done), channel_id=1, source_target_pairs={{0,1},{1,2},{2,3},{3,0},{4,5},{5,6},{6,7},{7,4},{8,9},{9,10},{10,1... | collective-permute-start | bytes 245768 | tf_op jit(solution)/shard_map/ppermute | solution.py:89
  75.4 3.9 %collective-permute-start.2 = (bf16[16,2,1280]{2,0,1:T(8,128)(2,1)S(1)}, bf16[16,2,1280]{2,0,1:T(8,128)(2,1)S(1)}, u32[]{:S(2)}, u32[]{:S(2)}) collective-permute-start(bf16[16,2,1280]{2,0,1:T(8,128)(2,1)S(1)} %collective-permute-done.1), channel_id=1, source_target_pairs={{0,1},{1,2},{2,3},{3,0},{4,5},{5,6},{6,7},{7,4},{8,9},{9,10},{10,1... | collective-permute-start | bytes 245768 | tf_op jit(solution)/shard_map/ppermute | solution.py:89
  84.3 0.8 copy-start.3
  88.2 1.7 %copy-start = (bf16[32,8,1280]{0,1,2:T(8,128)(2,1)S(1)}, bf16[32,8,1280]{0,1,2:T(8,128)(2,1)}, u32[]{:S(2)}) copy-start(bf16[32,8,1280]{0,1,2:T(8,128)(2,1)} %get-tuple-element.110) | copy-start | bytes 1966084 | tf_op jit(solution)/shard_map/while
  96.9 1.7 %copy-start.1 = (bf16[32,8,1280]{0,1,2:T(8,128)(2,1)S(1)}, bf16[32,8,1280]{0,1,2:T(8,128)(2,1)}, u32[]{:S(2)}) copy-start(bf16[32,8,1280]{0,1,2:T(8,128)(2,1)} %get-tuple-element.110) | copy-start | bytes 1966084 | tf_op jit(solution)/shard_map/while
  101.1 2.5 %copy-start.2 = (f32[8,32,640]{2,1,0:T(8,128)S(1)}, f32[8,32,640]{2,1,0:T(8,128)}, u32[]{:S(2)}) copy-start(f32[8,32,640]{2,1,0:T(8,128)} %copy.63) | copy-start | bytes 1966084 | tf_op jit(solution)/shard_map/while
  103.6 3.0 %copy-start.6 = (bf16[2,8,32,801]{3,2,1,0:T(8,128)(2,1)S(1)}, bf16[2,8,32,801]{3,2,1,0:T(8,128)(2,1)}, u32[]{:S(2)}) copy-start(bf16[2,8,32,801]{3,2,1,0:T(8,128)(2,1)} %get-tuple-element.102) | copy-start | bytes 2460676 | tf_op jit(solution)/shard_map/while
  103.6 4.0 %copy-start.4 = (bf16[2,8,8,1280]{3,2,1,0:T(8,128)(2,1)S(1)}, bf16[2,8,8,1280]{3,2,1,0:T(8,128)(2,1)}, u32[]{:S(2)}) copy-start(bf16[2,8,8,1280]{3,2,1,0:T(8,128)(2,1)} %copy-done.3) | copy-start | bytes 983044 | tf_op jit(solution)/shard_map/while
  106.7 0.9 copy-start.7
  107.6 0.8 copy-start.3
  111.5 1.7 %copy-start = (bf16[32,8,1280]{0,1,2:T(8,128)(2,1)S(1)}, bf16[32,8,1280]{0,1,2:T(8,128)(2,1)}, u32[]{:S(2)}) copy-start(bf16[32,8,1280]{0,1,2:T(8,128)(2,1)} %get-tuple-element.110) | copy-start | bytes 1966084 | tf_op jit(solution)/shard_map/while
  120.1 1.7 %copy-start.1 = (bf16[32,8,1280]{0,1,2:T(8,128)(2,1)S(1)}, bf16[32,8,1280]{0,1,2:T(8,128)(2,1)}, u32[]{:S(2)}) copy-start(bf16[32,8,1280]{0,1,2:T(8,128)(2,1)} %get-tuple-element.110) | copy-start | bytes 1966084 | tf_op jit(solution)/shard_map/while
  124.4 2.5 %copy-start.2 = (f32[8,32,640]{2,1,0:T(8,128)S(1)}, f32[8,32,640]{2,1,0:T(8,128)}, u32[]{:S(2)}) copy-start(f32[8,32,640]{2,1,0:T(8,128)} %copy.63) | copy-start | bytes 1966084 | tf_op jit(solution)/shard_map/while
  126.8 3.0 %copy-start.6 = (bf16[2,8,32,801]{3,2,1,0:T(8,128)(2,1)S(1)}, bf16[2,8,32,801]{3,2,1,0:T(8,128)(2,1)}, u32[]{:S(2)}) copy-start(bf16[2,8,32,801]{3,2,1,0:T(8,128)(2,1)} %get-tuple-element.102) | copy-start | bytes 2460676 | tf_op jit(solution)/shard_map/while
  126.9 4.0 %copy-start.4 = (bf16[2,8,8,1280]{3,2,1,0:T(8,128)(2,1)S(1)}, bf16[2,8,8,1280]{3,2,1,0:T(8,128)(2,1)}, u32[]{:S(2)}) copy-start(bf16[2,8,8,1280]{3,2,1,0:T(8,128)(2,1)} %copy-done.3) | copy-start | bytes 983044 | tf_op jit(solution)/shard_map/while
  129.9 0.9 copy-start.7
